TPU v7x, 32 devices: a whole 2x2x4 slice. The times are simulated.
32 devices in a mesh: seq: 8 (over z, x), tp: 4 (over y, core).
Axes of the slice: x: 2, y: 2, z: 4, core: 2. Of those that a mesh axis runs over, the one named last changes fastest.
Arguments:
- queries: bfloat16 [8192, 4096], P('seq', 'tp'), may hold values from -576 to 576
- group_cond: bfloat16 [128, 896], P('seq'), may hold values from -6 to 6
- nbr_shard: int32 [128, 2], P('seq'), may hold values from 0 to 7, all different within a row; in each aligned block of 16 rows (0 to 15, 16 to 31, ...) at most 4 rows name the same one
- nbr_row: int32 [128, 2], P('seq'), may hold values from 0 to 7
- database: bfloat16 [64, 16, 896], P('seq'), may hold values from -6 to 6
- enc_gain: bfloat16 [896], replicated, may hold values from 0.25 to 1.75
- w_in: bfloat16 [1792, 896], P('tp'), may hold values from -0.1875 to 0.1875
- w_out: bfloat16 [1792, 896], P('tp'), may hold values from -0.125 to 0.125
- w_kv: bfloat16 [2, 896, 4096], P(None, 'seq', 'tp'), may hold values from -0.1875 to 0.1875
Outputs:
- attended: bfloat16 [8192, 4096], P('seq', 'tp')
Inputs may be any that keep to these rules, and one draw needn't show every extreme that they name: `nbr_shard`: in each aligned block of 16 rows no shard is named by more than 4 rows, and one shard reaches 4; each row names 2 different shards.
All inputs are finite; a program needn't handle non-finite values.
Results may differ from a plain program's by a relative error of at most 0.025.
Values may be sent and summed in bfloat16 or wider, within the bound.
A program may use at most 64 MiB of HBM per device.

v0:
```python
import jax
import jax.numpy as jnp
from jax import lax
from jax.sharding import PartitionSpec as P

E = 896
HEAD = 128
GROUP = 64
K = 2
NL = 16


def slot_positions(shards, capacity):
    count = shards.shape[0]
    order = jnp.arange(count, dtype=jnp.int32)
    earlier = (shards[:, None] == shards[None, :]) & (order[None, :] < order[:, None])
    slot = jnp.sum(earlier.astype(jnp.int32), axis=1)
    return shards * capacity + slot


def request_table(positions, wanted, slot_total):
    match = positions[:, None] == jnp.arange(slot_total, dtype=jnp.int32)[None, :]
    return jnp.sum(jnp.where(match, wanted[:, None], 0), axis=0)


def body(queries, group_cond, nbr_shard, nbr_row, database, enc_gain, w_in, w_out, w_kv):
    seq_count = lax.axis_size("seq")
    group_count = nbr_shard.shape[0]
    capacity = (group_count * K + seq_count - 1) // seq_count
    slot_total = seq_count * capacity
    stored = database.shape[0]
    flat_shard = nbr_shard.reshape(-1)
    flat_row = nbr_row.reshape(-1)
    positions = slot_positions(flat_shard, capacity)
    table = request_table(positions, flat_row, slot_total).reshape(seq_count, capacity)
    store_flat = database.reshape(stored, NL * E)
    received = lax.all_to_all(table, "seq", split_axis=0, concat_axis=0, tiled=True)
    looked = jnp.take(store_flat, received.reshape(-1), axis=0)
    looked = looked.reshape(seq_count, received.shape[1], NL * E)
    replies = lax.all_to_all(looked, "seq", split_axis=0, concat_axis=0, tiled=True)
    raw_rows = jnp.take(replies.reshape(slot_total, NL * E), positions, axis=0)
    raw_rows = raw_rows.reshape(group_count, K, NL, E)
    summed_rows = (
        raw_rows.astype(jnp.float32) + group_cond.astype(jnp.float32)[:, None, None, :]
    ).astype(jnp.bfloat16)
    row_count = group_count * K * NL
    flat_rows = summed_rows.reshape(row_count, E).astype(jnp.float32)
    mean_square = jnp.mean(flat_rows * flat_rows, axis=1, keepdims=True)
    normed = (flat_rows * lax.rsqrt(mean_square + 1e-06) * enc_gain.astype(jnp.float32)).astype(
        jnp.bfloat16
    )
    pre_act = lax.dot_general(
        normed, w_in, (((1,), (1,)), ((), ())), preferred_element_type=jnp.float32
    )
    hidden = jax.nn.gelu(pre_act).astype(jnp.bfloat16)
    partial_out = jnp.dot(hidden, w_out, preferred_element_type=jnp.float32)
    ffn_out = lax.psum(partial_out, "tp")
    encoded = (flat_rows + ffn_out).astype(jnp.bfloat16)
    local_feat = w_kv.shape[2]
    piece = lax.all_gather(w_kv, "seq", axis=1, tiled=True)
    key_part = jnp.dot(encoded, piece[0], preferred_element_type=jnp.float32)
    value_part = jnp.dot(encoded, piece[1], preferred_element_type=jnp.float32)
    local_heads = local_feat // HEAD
    keys = key_part.astype(jnp.bfloat16).reshape(group_count, K * NL, local_heads, HEAD)
    values = value_part.astype(jnp.bfloat16).reshape(group_count, K * NL, local_heads, HEAD)
    query_blocks = queries.reshape(group_count, GROUP, local_heads, HEAD)
    scores = jnp.einsum("cqhd,ckhd->chqk", query_blocks, keys, preferred_element_type=jnp.float32)
    scores = scores / jnp.sqrt(jnp.float32(HEAD))
    weights = jax.nn.softmax(scores, axis=-1).astype(jnp.bfloat16)
    attended = jnp.einsum("chqk,ckhd->cqhd", weights, values, preferred_element_type=jnp.float32)
    return attended.astype(jnp.bfloat16).reshape(group_count * GROUP, local_feat)


def solution(mesh):
    placed = (
        P("seq", "tp"),
        P("seq", None),
        P("seq", None),
        P("seq", None),
        P("seq", None, None),
        P(),
        P("tp", None),
        P("tp", None),
        P(None, "seq", "tp"),
    )
    return jax.shard_map(
        body, mesh=mesh, in_specs=placed, out_specs=P("seq", "tp"), check_vma=False
    )
```

profile of v0, /device:TPU:0, one launch (start us, length us, event | category | flops | bytes accessed | tf_op | source)
XLA Modules:
  0.0 152.0 jit_solution(6324980175791629989)
XLA Ops:
  7.4 0.8 copy.37
  8.2 0.1 reshape.154
  8.3 0.2 convert_reduce_fusion
  8.5 0.8 copy.39
  9.2 0.1 broadcast_in_dim.54
  9.3 0.1 select_reduce_fusion
  9.4 0.7 all_to_all.9
  10.1 7.3 %all-to-all-start = ((s32[8,1,4]{2,1,0:T(1,128)}), s32[8,1,4]{2,1,0:T(1,128)S(1)}, u32[]{:S(2)}, u32[]{:S(2)}) async-start(s32[8,1,4]{2,1,0:T(1,128)} %bitcast), calls=%async_computation | async-start | bytes 8192 | tf_op jit(solution)/shard_map/all_to_all | solution.py:37
  17.4 1.0 copy.47
  18.3 5.4 %all-to-all-done = s32[8,1,4]{2,1,0:T(1,128)S(1)} async-done(((s32[8,1,4]{2,1,0:T(1,128)}), s32[8,1,4]{2,1,0:T(1,128)S(1)}, u32[]{:S(2)}, u32[]{:S(2)}) %all-to-all-start) | async-done | bytes 160 | tf_op jit(solution)/shard_map/all_to_all | solution.py:37
  23.8 0.5 broadcast.119
  24.4 0.7 reduce.4
  25.1 0.1 copy.42
  25.2 1.1 gather_fusion
  26.3 0.3 gather.15
  26.7 1.4 broadcast_select_fusion
  28.1 3.6 %all-to-all-start.1 = ((bf16[8,4,14336]{2,1,0:T(4,128)(2,1)}), bf16[8,4,14336]{2,1,0:T(4,128)(2,1)S(1)}, u32[]{:S(2)}, u32[]{:S(2)}) async-start(bf16[8,4,14336]{2,1,0:T(4,128)(2,1)} %broadcast_select_fusion), calls=%async_computation.1 | async-start | bytes 1835008 | tf_op jit(solution)/shard_map/all_to_all | solution.py:40
  31.8 0.6 convert_element_type.61
  32.4 0.1 mul.71
  32.5 0.1 broadcast_in_dim.51
  32.6 0.6 broadcast_in_dim.52
  33.2 0.6 convert_element_type.55
  33.9 0.6 pad_clamp_fusion
  34.5 19.1 %all-to-all-done.1 = bf16[8,4,14336]{2,1,0:T(4,128)(2,1)S(1)} async-done(((bf16[8,4,14336]{2,1,0:T(4,128)(2,1)}), bf16[8,4,14336]{2,1,0:T(4,128)(2,1)S(1)}, u32[]{:S(2)}, u32[]{:S(2)}) %all-to-all-start.1) | async-done | bytes 917536 | tf_op jit(solution)/shard_map/all_to_all | solution.py:40
  53.6 0.2 reshape.158
  53.8 1.2 gather_fusion.1
  55.1 0.4 gather.17
  55.5 0.1 copy.48
  55.6 0.2 copy-done.3
  55.9 0.4 multiply_reduce_fusion
  56.3 0.1 rsqrt.12
  56.4 0.3 fusion.13
  56.8 2.7 %fusion.35 = f32[512,896]{1,0:T(8,128)} fusion(bf16[448,896]{1,0:T(8,128)(2,1)S(1)} %copy-done, bf16[448,896]{1,0:T(8,128)(2,1)S(1)} %copy-done.12, bf16[512,896]{1,0:T(8,128)(2,1)S(1)} %fusion.13, f32[896]{0:T(1024)S(1)} %copy-done.7, f32[512]{0:T(512)S(1)} %rsqrt.12), kind=kOutput, calls=%fused_computation.44 | convolution fusion | flops 825982976 | bytes 4363776 | tf_op jit(solution)/shard_map/dot_general | solution.py:56
  59.5 0.2 all-gather.2.cloned.1.call-start
  59.7 0.3 all-gather.2.cloned.1.call-update
  60.1 2.2 %copy.51 = bf16[128,8,8,128]{3,2,1,0:T(8,128)(2,1)S(1)} copy(bf16[128,8,8,128]{3,1,2,0:T(8,128)(2,1)} %bitcast.73) | data formatting | bytes 4194304
  62.3 43.4 %all-reduce.2.cloned.1.call-done = f32[512,896]{1,0:T(8,128)} async-done(((f32[512,896]{1,0:T(8,128)}), f32[512,896]{1,0:T(8,128)}) %all-reduce.2.cloned.1.call-update) | async-done | bytes 1835024 | tf_op jit(solution)/shard_map/psum | solution.py:57
  105.7 21.7 %all-gather.2.cloned.1.call-done = bf16[2,896,1024]{2,1,0:T(8,128)(2,1)} async-done(((bf16[2,112,1024]{2,1,0:T(8,128)(2,1)}), bf16[2,896,1024]{2,1,0:T(8,128)(2,1)}) %all-gather.2.cloned.1.call-update) | async-done | bytes 3670032 | tf_op jit(solution)/shard_map/all_gather | solution.py:60
  127.4 3.7 %fusion.17 = bf16[64,8,8,128]{3,1,2,0:T(8,128)(2,1)S(1)} fusion(bf16[2,896,1024]{2,1,0:T(8,128)(2,1)} %all-gather.2.cloned.1.call-done, f32[512,896]{1,0:T(8,128)} %all-reduce.2.cloned.1.call-done, bf16[512,896]{1,0:T(8,128)(2,1)} %copy-done.1), kind=kOutput, calls=%fused_computation.30 | convolution fusion | flops 941424640 | bytes 5636096 | tf_op jit(solution)/shard_map/dot_general | solution.py:62
  131.2 0.3 copy.49
  131.5 0.9 copy-done.2
  132.4 1.3 fusion.16
  133.7 0.3 copy.50
  134.0 1.2 fusion.3
  135.2 4.8 %fusion.55 = (f32[16,8,64]{2,1,0:T(8,128)S(1)}, f32[16,8,64,32]{2,3,1,0:T(8,128)S(1)}) fusion(f32[16,8,32,64]{3,2,1,0:T(8,128)S(1)} %fusion.3), kind=kOutput, calls=%fused_computation.76 | output fusion | flops 1048607 | bytes 2129920 | tf_op jit(solution)/shard_map/sub | solution.py:69
  140.0 0.8 convert_bitcast_fusion
  140.8 1.8 %copy.46 = bf16[16,64,8,128]{3,2,1,0:T(8,128)(2,1)S(1)} copy(bf16[16,64,8,128]{3,1,2,0:T(8,128)(2,1)S(1)} %convert_bitcast_fusion) | data formatting | bytes 4194304 | tf_op jit(solution)/shard_map/convert_element_type | solution.py:71
  142.6 1.9 %copy.60 = bf16[128,8,8,128]{3,1,2,0:T(8,128)(2,1)} copy(bf16[128,8,8,128]{3,2,1,0:T(8,128)(2,1)S(1)} %bitcast.69) | data formatting | bytes 4194304
  (37 shorter events, 0.4 us)
Async XLA Ops:
  7.4 49.4 %copy-start = (bf16[448,896]{1,0:T(8,128)(2,1)S(1)}, bf16[448,896]{1,0:T(8,128)(2,1)}, u32[]{:S(2)}) copy-start(bf16[448,896]{1,0:T(8,128)(2,1)} %param.16) | copy-start | bytes 2408452
  10.1 13.6 %all-to-all-start = ((s32[8,1,4]{2,1,0:T(1,128)}), s32[8,1,4]{2,1,0:T(1,128)S(1)}, u32[]{:S(2)}, u32[]{:S(2)}) async-start(s32[8,1,4]{2,1,0:T(1,128)} %bitcast), calls=%async_computation | async-start | bytes 8192 | tf_op jit(solution)/shard_map/all_to_all | solution.py:37
  26.7 5.1 %copy-start.9 = (bf16[896]{0:T(1024)(128)(2,1)S(1)}, bf16[896]{0:T(1024)(128)(2,1)}, u32[]{:S(2)}) copy-start(bf16[896]{0:T(1024)(128)(2,1)} %param.14) | copy-start | bytes 5380
  26.7 6.5 %copy-start.4 = (bf16[16,896]{1,0:T(8,128)(2,1)S(1)}, bf16[16,896]{1,0:T(8,128)(2,1)}, u32[]{:S(2)}) copy-start(bf16[16,896]{1,0:T(8,128)(2,1)} %param.10) | copy-start | bytes 86020
  28.1 25.5 %all-to-all-start.1 = ((bf16[8,4,14336]{2,1,0:T(4,128)(2,1)}), bf16[8,4,14336]{2,1,0:T(4,128)(2,1)S(1)}, u32[]{:S(2)}, u32[]{:S(2)}) async-start(bf16[8,4,14336]{2,1,0:T(4,128)(2,1)} %broadcast_select_fusion), calls=%async_computation.1 | async-start | bytes 1835008 | tf_op jit(solution)/shard_map/all_to_all | solution.py:40
  31.7 74.0 %all-reduce.2.cloned.1.call-start = ((), (), s32[]{:S(2)}) async-start(), calls=%async_computation.2 | async-start | bytes 3670016 | tf_op jit(solution)/shard_map/psum | solution.py:57
  32.5 21.1 %copy-start.5 = (pred[16,2]{1,0:T(8,128)(4,1)}, pred[16,2]{1,0:T(8,128)(4,1)S(1)}, u32[]{:S(2)}) copy-start(pred[16,2]{1,0:T(8,128)(4,1)S(1)} %compare_and_fusion) | copy-start | bytes 100
  55.0 0.8 copy-start.3
  55.0 0.8 copy-start.6
  55.1 1.4 copy-start.8
  55.5 1.2 copy-start.7
  55.5 1.2 copy-start.12
  56.8 2.7 %copy-start.1 = (bf16[512,896]{1,0:T(8,128)(2,1)}, bf16[512,896]{1,0:T(8,128)(2,1)S(1)}, u32[]{:S(2)}) copy-start(bf16[512,896]{1,0:T(8,128)(2,1)S(1)} %fusion.13) | copy-start | bytes 2752516
  59.5 67.9 %all-gather.2.cloned.1.call-start = ((), (), s32[]{:S(2)}) async-start(), calls=%async_computation.3 | async-start | bytes 4128768 | tf_op jit(solution)/shard_map/all_gather | solution.py:60
  127.4 4.0 %copy-start.10 = (bf16[2,896,1024]{2,1,0:T(8,128)(2,1)S(1)}, bf16[2,896,1024]{2,1,0:T(8,128)(2,1)}, u32[]{:S(2)}) copy-start(bf16[2,896,1024]{2,1,0:T(8,128)(2,1)} %all-gather.2.cloned.1.call-done) | copy-start | bytes 11010052
  127.4 4.0 %copy-start.11 = (f32[512,896]{1,0:T(8,128)S(1)}, f32[512,896]{1,0:T(8,128)}, u32[]{:S(2)}) copy-start(f32[512,896]{1,0:T(8,128)} %all-reduce.2.cloned.1.call-done) | copy-start | bytes 5505028
  131.2 1.2 copy-start.2
Sparse Core Ops, SparseCore 0:
  59.6 46.0 all-reduce.1
Sparse Core Ops, SparseCore 1:
  62.2 65.2 all-gather.1
where the time goes:
time: 152 us
  waiting for transfers between devices  90 us (59%)
  local copies, waits for them, and re-layouts  16.3 us (11%)
  between operations  15.2 us (10%)
  starting transfers between devices  11.1 us (7%)
  other arithmetic  9.75 us (6%)
  matrix products  9.71 us (6%)
    psum x1, waiting for transfers between devices, body(): ffn_out = lax.psum(partial_out, 'tp')  43.4 us
    all_gather x1, waiting for transfers between devices, body(): piece = lax.all_gather(w_kv, 'seq', axis=1, tiled=True)  21.7 us
    all_to_all x1, waiting for transfers between devices, body(): lax.all_to_all(looked, 'seq', split_axis=0, concat_axis=0, tiled=True)  19.1 us
    unnamed x34, local copies, waits for them, and re-layouts  8.58 us
    all_to_all x1, starting transfers between devices, body(): lax.all_to_all(table, 'seq', split_axis=0, concat_axis=0, tiled=True)  7.25 us
    all_to_all x1, waiting for transfers between devices, body(): lax.all_to_all(table, 'seq', split_axis=0, concat_axis=0, tiled=True)  5.41 us
    sub x1, other arithmetic, body(): weights = jax.nn.softmax(scores, axis=-1).astype(jnp.bfloat16)  4.81 us
    dot_general x1, matrix products, body(): value_part = jnp.dot(encoded, piece[1], preferred_element_type=jnp.float32)  3.73 us
  transfers between devices with their start and end apart: 4, of which 4 were waited for; matrix products, arithmetic and copies ran while one was open for 4% of the time, Pallas kernels for 0%

commit v1 on v0

--- a/solution.py
+++ b/solution.py
@@ -1,6 +1,8 @@
 import jax
 import jax.numpy as jnp
 from jax import lax
+from jax.experimental import pallas as pl
+from jax.experimental.pallas import tpu as pltpu
 from jax.sharding import PartitionSpec as P
 
 E = 896
@@ -70,6 +72,392 @@
     attended = jnp.einsum("chqk,ckhd->cqhd", weights, values, preferred_element_type=jnp.float32)
     return attended.astype(jnp.bfloat16).reshape(group_count * GROUP, local_feat)
 
+MESH = pl.DeviceIdType.MESH
+ACROSS = 4
+PIECES = 8
+WIDE = 256
+
+
+def fused_kernel(
+    queries_hbm, cond_ref, shard_ref, row_ref, db_ref, gain_ref, w_in_hbm, w_out_hbm, w_kv_ref,
+    out_ref,
+    wbuf, dbp, condf, xs, xv, nv, enc, part_send, part_recv, own_sum, y_send, y_recv,
+    q_ref, w_in_ref, w_out_ref,
+    local_sem, db_send, db_recv, w_send, w_recv, xs_send, xs_recv, sum_send, sum_recv,
+):
+    s = lax.axis_index("seq")
+    t = lax.axis_index("tp")
+    z, x = s // 2, s % 2
+    core = t % 2
+    flip = s + 1 - 2 * x
+    sib = t + 1 - 2 * core
+    ypeer = (t + 2) % 4
+    stored = db_ref.shape[0]
+    depth = w_kv_ref.shape[1]
+    rows = enc.shape[0]
+    half = rows // 2
+    e = enc.shape[1]
+    off = pl.multiple_of(jnp.minimum(t * WIDE, e - WIDE), 128)
+
+    barrier = pltpu.get_barrier_semaphore()
+    for i in range(1, 8):
+        pl.semaphore_signal(barrier, inc=1, device_id=((s + i) % 8, t), device_id_type=MESH)
+    pl.semaphore_signal(barrier, inc=1, device_id=(s, sib), device_id_type=MESH)
+    pl.semaphore_signal(barrier, inc=1, device_id=(s, ypeer), device_id_type=MESH)
+    loads = [
+        pltpu.make_async_copy(w_in_hbm, w_in_ref, local_sem.at[0]),
+        pltpu.make_async_copy(w_out_hbm, w_out_ref, local_sem.at[1]),
+        pltpu.make_async_copy(queries_hbm, q_ref, local_sem.at[2]),
+    ]
+    for load in loads:
+        load.start()
+    pl.semaphore_wait(barrier, 9)
+
+    def db_copy(i):
+        return pltpu.make_async_remote_copy(
+            src_ref=db_ref.at[:, :, pl.ds(off, WIDE)],
+            dst_ref=dbp.at[pl.ds(s * stored, stored)],
+            send_sem=db_send.at[i],
+            recv_sem=db_recv.at[i],
+            device_id=((s + i) % 8, t),
+            device_id_type=MESH,
+        )
+
+    def db_arrival(i):
+        source = (s + 8 - i) % 8
+        return pltpu.make_async_copy(
+            dbp.at[pl.ds(source * stored, stored)], dbp.at[pl.ds(source * stored, stored)], db_recv.at[i]
+        )
+
+    for i in range(1, 8):
+        db_copy(i).start()
+
+    def slot(p, b):
+        return wbuf.at[p, pl.ds(pl.multiple_of(b * depth, 16), depth), :]
+
+    def own_piece(p):
+        return w_kv_ref.at[p % 2, :, pl.ds(pl.multiple_of((p // 2) * WIDE, WIDE), WIDE)]
+
+    def w_copy(src, p, b, way):
+        target = (flip, s + 2, s - 2)[way]
+        return pltpu.make_async_remote_copy(
+            src_ref=src,
+            dst_ref=slot(p, b),
+            send_sem=w_send.at[way, p, b],
+            recv_sem=w_recv.at[p, b],
+            device_id=(target, t),
+            device_id_type=MESH,
+        )
+
+    def w_arrival(p, b):
+        return pltpu.make_async_copy(slot(p, b), slot(p, b), w_recv.at[p, b])
+
+    def own_start(p, carry):
+        w_copy(own_piece(p), p, s, 0).start()
+
+        @pl.when(z < ACROSS - 1)
+        def _():
+            w_copy(own_piece(p), p, s, 1).start()
+
+        @pl.when(z > 0)
+        def _():
+            w_copy(own_piece(p), p, s, 2).start()
+
+        pltpu.make_async_copy(own_piece(p), slot(p, s), w_recv.at[p, s]).start()
+        return carry
+
+    lax.fori_loop(0, PIECES, own_start, 0)
+
+    def pass_on(hop, first, last):
+        def one(p, carry):
+            @pl.when(z >= hop)
+            def _():
+                b = s - 2 * hop
+                w_arrival(p, b).wait()
+                w_copy(slot(p, b), p, b, 0).start()
+
+                @pl.when(z < ACROSS - 1)
+                def _():
+                    w_copy(slot(p, b), p, b, 1).start()
+
+            @pl.when(z + hop < ACROSS)
+            def _():
+                b = s + 2 * hop
+                w_arrival(p, b).wait()
+                w_copy(slot(p, b), p, b, 0).start()
+
+                @pl.when(z > 0)
+                def _():
+                    w_copy(slot(p, b), p, b, 2).start()
+
+            return carry
+
+        lax.fori_loop(first, last, one, 0)
+
+    condf[...] = cond_ref[:, pl.ds(off, WIDE)].astype(jnp.float32)
+    dbp[pl.ds(s * stored, stored)] = db_ref[:, :, pl.ds(off, WIDE)]
+    for i in range(1, 8):
+        db_arrival(i).wait()
+
+    def pick(g, carry):
+        for k in range(K):
+            at = shard_ref[g, k] * stored + row_ref[g, k]
+            picked = dbp[at].astype(jnp.float32) + condf[pl.ds(g, 1), :]
+            xs[t, pl.ds(pl.multiple_of((g * K + k) * NL, NL), NL), :] = picked.astype(jnp.bfloat16)
+        return carry
+
+    lax.fori_loop(0, rows // (K * NL), pick, 0)
+
+    def xs_copy(quarter, target, number):
+        return pltpu.make_async_remote_copy(
+            src_ref=xs.at[quarter],
+            dst_ref=xs.at[quarter],
+            send_sem=xs_send.at[number],
+            recv_sem=xs_recv.at[quarter],
+            device_id=(s, target),
+            device_id_type=MESH,
+        )
+
+    def xs_arrival(quarter):
+        return pltpu.make_async_copy(xs.at[quarter], xs.at[quarter], xs_recv.at[quarter])
+
+    xs_copy(t, ypeer, 0).start()
+    xs_copy(t, sib, 1).start()
+    pass_on(1, 0, PIECES // 2)
+    xs_arrival(ypeer).wait()
+    xs_copy(ypeer, sib, 2).start()
+    pass_on(1, PIECES // 2, PIECES)
+    xs_arrival(sib).wait()
+    xs_arrival((sib + 2) % 4).wait()
+
+    gain = gain_ref[...].astype(jnp.float32)
+
+    def norm(i, carry):
+        at = pl.ds(pl.multiple_of(i * 64, 64), 64)
+        whole = jnp.concatenate(
+            [xs[0, at, :], xs[1, at, :], xs[2, at, :], xs[3, at, pl.ds(4 * WIDE - e, e - 3 * WIDE)]], axis=1
+        )
+        xv[at, :] = whole
+        wide = whole.astype(jnp.float32)
+        mean_square = jnp.mean(wide * wide, axis=1, keepdims=True)
+        nv[at, :] = (wide * lax.rsqrt(mean_square + 1e-06) * gain).astype(jnp.bfloat16)
+        return carry
+
+    lax.fori_loop(0, rows // 64, norm, 0)
+    loads[0].wait()
+    loads[1].wait()
+
+    def ffn(first):
+        block = nv[pl.ds(pl.multiple_of(first, 128), 128), :]
+        pre_act = lax.dot_general(
+            block, w_in_ref[...], (((1,), (1,)), ((), ())), preferred_element_type=jnp.float32
+        )
+        hidden = jax.nn.gelu(pre_act).astype(jnp.bfloat16)
+        return jnp.dot(hidden, w_out_ref[...], preferred_element_type=jnp.float32)
+
+    def sum_copy(src, dst, target, number):
+        return pltpu.make_async_remote_copy(
+            src_ref=src,
+            dst_ref=dst,
+            send_sem=sum_send.at[number],
+            recv_sem=sum_recv.at[number],
+            device_id=(s, target),
+            device_id_type=MESH,
+        )
+
+    theirs = (1 - core) * half
+    mine = core * half
+    steps = half // 128
+
+    def at_row(i):
+        return pl.ds(pl.multiple_of(i * 128, 128), 128)
+
+    def to_sib(i):
+        return sum_copy(part_send.at[at_row(i)], part_recv.at[at_row(i)], sib, i)
+
+    def to_y(i):
+        return sum_copy(y_send.at[at_row(i)], y_recv.at[at_row(i)], ypeer, steps + i)
+
+    def to_share(i):
+        where = pl.ds(pl.multiple_of(mine + i * 128, 128), 128)
+        return sum_copy(enc.at[where], enc.at[where], sib, 2 * steps + i)
+
+    def share_arrival(i):
+        where = pl.ds(pl.multiple_of(theirs + i * 128, 128), 128)
+        return pltpu.make_async_copy(enc.at[where], enc.at[where], sum_recv.at[2 * steps + i])
+
+    def send_theirs(i, carry):
+        part_send[at_row(i), :] = ffn(theirs + i * 128).astype(jnp.bfloat16)
+        to_sib(i).start()
+        return carry
+
+    lax.fori_loop(0, steps, send_theirs, 0)
+
+    def send_mine(i, carry):
+        own = ffn(mine + i * 128)
+        to_sib(i).wait_recv()
+        own = own + part_recv[at_row(i), :].astype(jnp.float32)
+        own_sum[at_row(i), :] = own
+        y_send[at_row(i), :] = own.astype(jnp.bfloat16)
+        to_y(i).start()
+        return carry
+
+    lax.fori_loop(0, steps, send_mine, 0)
+    pass_on(2, 0, PIECES)
+
+    def share_mine(i, carry):
+        where = pl.ds(pl.multiple_of(mine + i * 128, 128), 128)
+        to_y(i).wait_recv()
+        total = own_sum[at_row(i), :] + y_recv[at_row(i), :].astype(jnp.float32)
+        enc[where, :] = (xv[where, :].astype(jnp.float32) + total).astype(jnp.bfloat16)
+        to_share(i).start()
+        return carry
+
+    lax.fori_loop(0, steps, share_mine, 0)
+    pass_on(3, 0, PIECES)
+
+    def await_share(i, carry):
+        share_arrival(i).wait()
+        return carry
+
+    lax.fori_loop(0, steps, await_share, 0)
+    loads[2].wait()
+
+    span = 4 * K * NL
+    qspan = 4 * GROUP
+    tall = lax.broadcasted_iota(jnp.int32, (qspan, span), 0) // GROUP
+    flat = lax.broadcasted_iota(jnp.int32, (qspan, span), 1) // (K * NL)
+    inside = tall == flat
+    scale = HEAD ** -0.5
+    ones = jnp.ones((span, HEAD), jnp.bfloat16)
+
+    def chunk(c, carry):
+        for j in range(2):
+            p = 2 * c + j
+            pltpu.make_async_copy(own_piece(p), slot(p, s), w_recv.at[p, s]).wait()
+            for i in range(ACROSS):
+                w_arrival(p, 2 * i + 1 - x).wait()
+
+        def quad(i, inner):
+            krows = pl.ds(pl.multiple_of(i * span, span), span)
+            qrows = pl.ds(pl.multiple_of(i * qspan, qspan), qspan)
+            block = enc[krows, :]
+            keys = jnp.dot(block, wbuf[2 * c], preferred_element_type=jnp.float32).astype(jnp.bfloat16)
+            values = jnp.dot(block, wbuf[2 * c + 1], preferred_element_type=jnp.float32).astype(jnp.bfloat16)
+            for h in range(WIDE // HEAD):
+                cols = pl.ds(pl.multiple_of(c * WIDE + h * HEAD, HEAD), HEAD)
+                query = q_ref[qrows, cols]
+                scores = lax.dot_general(
+                    query, keys[:, h * HEAD : (h + 1) * HEAD], (((1,), (1,)), ((), ())),
+                    preferred_element_type=jnp.float32,
+                )
+                scores = jnp.where(inside, scores * scale, -jnp.inf)
+                top = jnp.max(scores, axis=1, keepdims=True)
+                grown = jnp.exp(scores - top).astype(jnp.bfloat16)
+                both = jnp.concatenate([values[:, h * HEAD : (h + 1) * HEAD], ones], axis=1)
+                mixed = jnp.dot(grown, both, preferred_element_type=jnp.float32)
+                out_ref[qrows, cols] = (mixed[:, :HEAD] / mixed[:, HEAD:]).astype(jnp.bfloat16)
+            return inner
+
+        lax.fori_loop(0, rows // span, quad, 0)
+        return carry
+
+    lax.fori_loop(0, PIECES // 2, chunk, 0)
+
+    for i in range(1, 8):
+        db_copy(i).wait_send()
+    xs_copy(t, ypeer, 0).wait_send()
+    xs_copy(t, sib, 1).wait_send()
+    xs_copy(ypeer, sib, 2).wait_send()
+
+    def sums_done(i, carry):
+        to_sib(i).wait_send()
+        to_y(i).wait_send()
+        to_share(i).wait_send()
+        return carry
+
+    lax.fori_loop(0, steps, sums_done, 0)
+
+    def sends_done(p, carry):
+        w_copy(own_piece(p), p, s, 0).wait_send()
+
+        @pl.when(z < ACROSS - 1)
+        def _():
+            w_copy(own_piece(p), p, s, 1).wait_send()
+
+        @pl.when(z > 0)
+        def _():
+            w_copy(own_piece(p), p, s, 2).wait_send()
+
+        for hop in range(1, ACROSS):
+            @pl.when(z >= hop)
+            def _():
+                b = s - 2 * hop
+                w_copy(slot(p, b), p, b, 0).wait_send()
+
+                @pl.when(z < ACROSS - 1)
+                def _():
+                    w_copy(slot(p, b), p, b, 1).wait_send()
+
+            @pl.when(z + hop < ACROSS)
+            def _():
+                b = s + 2 * hop
+                w_copy(slot(p, b), p, b, 0).wait_send()
+
+                @pl.when(z > 0)
+                def _():
+                    w_copy(slot(p, b), p, b, 2).wait_send()
+
+        return carry
+
+    lax.fori_loop(0, PIECES, sends_done, 0)
+
+
+def fused_body(queries, group_cond, nbr_shard, nbr_row, database, enc_gain, w_in, w_out, w_kv):
+    bf16, f32 = jnp.bfloat16, jnp.float32
+    rows = nbr_shard.shape[0] * K * NL
+    half = rows // 2
+    steps = half // 128
+    vmem = pl.BlockSpec(memory_space=pltpu.VMEM)
+    smem = pl.BlockSpec(memory_space=pltpu.SMEM)
+    anywhere = pl.BlockSpec(memory_space=pl.ANY)
+    dma = pltpu.SemaphoreType.DMA
+    return pl.pallas_call(
+        fused_kernel,
+        out_shape=jax.ShapeDtypeStruct(queries.shape, bf16),
+        in_specs=[anywhere, vmem, smem, smem, vmem, vmem, anywhere, anywhere, vmem],
+        out_specs=vmem,
+        scratch_shapes=[
+            pltpu.VMEM((PIECES, E, WIDE), bf16),
+            pltpu.VMEM((8 * database.shape[0], NL, WIDE), bf16),
+            pltpu.VMEM((group_cond.shape[0], WIDE), f32),
+            pltpu.VMEM((4, rows, WIDE), bf16),
+            pltpu.VMEM((rows, E), bf16),
+            pltpu.VMEM((rows, E), bf16),
+            pltpu.VMEM((rows, E), bf16),
+            pltpu.VMEM((half, E), bf16),
+            pltpu.VMEM((half, E), bf16),
+            pltpu.VMEM((half, E), f32),
+            pltpu.VMEM((half, E), bf16),
+            pltpu.VMEM((half, E), bf16),
+            pltpu.VMEM(queries.shape, bf16),
+            pltpu.VMEM(w_in.shape, bf16),
+            pltpu.VMEM(w_out.shape, bf16),
+            dma((3,)),
+            dma((8,)),
+            dma((8,)),
+            dma((3, PIECES, 8)),
+            dma((PIECES, 8)),
+            dma((3,)),
+            dma((4,)),
+            dma((3 * steps,)),
+            dma((3 * steps,)),
+        ],
+        compiler_params=pltpu.CompilerParams(
+            collective_id=0, has_side_effects=True, vmem_limit_bytes=40 * 1024 * 1024
+        ),
+    )(queries, group_cond, nbr_shard, nbr_row, database, enc_gain.reshape(1, E), w_in, w_out, w_kv)
+
 
 def solution(mesh):
     placed = (
@@ -83,6 +471,7 @@
         P("tp", None),
         P(None, "seq", "tp"),
     )
+    fused = mesh.shape["seq"] == 8 and mesh.shape["tp"] == 4
     return jax.shard_map(
-        body, mesh=mesh, in_specs=placed, out_specs=P("seq", "tp"), check_vma=False
+        fused_body if fused else body, mesh=mesh, in_specs=placed, out_specs=P("seq", "tp"), check_vma=False
     )

time: 152 us -> 71.7 us (0.47)
  waiting for transfers between devices: 90 us -> 0 us
  Pallas kernels: 0 us -> 61.2 us
  between operations: 15.2 us -> 0.02 us
  starting transfers between devices: 11.1 us -> 0 us
  other arithmetic: 9.75 us -> 0 us
  matrix products: 9.71 us -> 0 us
  local copies, waits for them, and re-layouts: 16.3 us -> 10.1 us
    pallas_call x0 -> x1, Pallas kernels: none -> 61.2 us  [fused_body(): pl.pallas_call(fused_kernel, out_shape=jax.ShapeDtypeStruct(queries.shape...]
    psum x1 -> x0, waiting for transfers between devices: 43.4 us -> none  [body(): ffn_out = lax.psum(partial_out, 'tp')]
    all_to_all x2 -> x0, waiting for transfers between devices: 24.5 us -> none  [the longest x1 19.1 us: body(): lax.all_to_all(looked, 'seq', split_axis=0, concat_axis=0, tiled=True)]
    all_gather x1 -> x0, waiting for transfers between devices: 21.7 us -> none  [body(): piece = lax.all_gather(w_kv, 'seq', axis=1, tiled=True)]
    all_to_all x2 -> x0, starting transfers between devices: 10.8 us -> none  [the longest x1 7.25 us: body(): lax.all_to_all(table, 'seq', split_axis=0, concat_axis=0, tiled=True)]
    dot_general x5 -> x0, matrix products: 9.71 us -> none  [the longest x1 3.73 us: body(): value_part = jnp.dot(encoded, piece[1], preferred_element_type=jnp.float32)]
    sub x1 -> x0, other arithmetic: 4.81 us -> none  [body(): weights = jax.nn.softmax(scores, axis=-1).astype(jnp.bfloat16)]
    gather x4 -> x0, local copies, waits for them, and re-layouts: 3.12 us -> none  [the longest x2 1.66 us: body(): raw_rows = jnp.take(replies.reshape(slot_total, NL * E), positions, axis=0)]
  transfers between devices with their start and end apart: 4 -> 0, of which waited for: 4 -> 0; matrix products, arithmetic and copies ran while one was open for 4% -> 0% of each run, Pallas kernels for 0% -> 0%
where the time goes in v1:
time: 71.7 us; the launch traced here: 71.3 us
  Pallas kernels  61.2 us (85%)
  local copies, waits for them, and re-layouts  10.1 us (14%)
    pallas_call x1, Pallas kernels, fused_body(): pl.pallas_call(fused_kernel, out_shape=jax.ShapeDtypeStruct(queries.shape...  61.2 us
    unnamed x15, local copies, waits for them, and re-layouts  9.4 us

profile of v1, /device:TPU:0, one launch (start us, length us, event | category | flops | bytes accessed | tf_op | source)
XLA Modules:
  0.0 71.3 jit_solution(7267139927217716841)
XLA Ops:
  0.0 0.7 reshape.3.gain_ref
  0.7 0.8 %copy.10.shard_ref = s32[16,2]{1,0:T(8,128)S(1)} copy(s32[16,2]{0,1:T(2,128)} %param.11) | data formatting | bytes 256 | tf_op args[2]
  1.4 0.8 %copy.11.row_ref = s32[16,2]{1,0:T(8,128)S(1)} copy(s32[16,2]{0,1:T(2,128)} %param.12) | data formatting | bytes 256 | tf_op args[3]
  2.2 0.0 copy-start
  2.2 1.6 %copy-done = bf16[1024,1024]{1,0:T(8,128)(2,1)S(1)} copy-done((bf16[1024,1024]{1,0:T(8,128)(2,1)S(1)}, bf16[1024,1024]{1,0:T(8,128)(2,1)}, u32[]{:S(2)}) %copy-start) | copy-done | bytes 2097176
  3.8 0.0 copy-start.1
  3.8 1.1 %copy-done.1 = bf16[448,896]{1,0:T(8,128)(2,1)S(1)} copy-done((bf16[448,896]{1,0:T(8,128)(2,1)S(1)}, bf16[448,896]{1,0:T(8,128)(2,1)}, u32[]{:S(2)}) %copy-start.1) | copy-done | bytes 802840
  4.9 0.0 copy-start.2
  4.9 1.1 %copy-done.2 = bf16[448,896]{1,0:T(8,128)(2,1)S(1)} copy-done((bf16[448,896]{1,0:T(8,128)(2,1)S(1)}, bf16[448,896]{1,0:T(8,128)(2,1)}, u32[]{:S(2)}) %copy-start.2) | copy-done | bytes 802840
  6.1 0.0 copy-start.3
  6.1 1.0 %copy-done.3 = bf16[2,112,1024]{2,1,0:T(8,128)(2,1)S(1)} copy-done((bf16[2,112,1024]{2,1,0:T(8,128)(2,1)S(1)}, bf16[2,112,1024]{2,1,0:T(8,128)(2,1)}, u32[]{:S(2)}) %copy-start.3) | copy-done | bytes 458776
  7.1 0.0 copy-start.4
  7.1 0.9 %copy-done.4 = bf16[8,16,896]{2,1,0:T(8,128)(2,1)S(1)} copy-done((bf16[8,16,896]{2,1,0:T(8,128)(2,1)S(1)}, bf16[8,16,896]{2,1,0:T(8,128)(2,1)}, u32[]{:S(2)}) %copy-start.4) | copy-done | bytes 229400
  8.0 0.0 copy-start.5
  8.0 0.7 %copy-done.5 = bf16[16,896]{1,0:T(8,128)(2,1)S(1)} copy-done((bf16[16,896]{1,0:T(8,128)(2,1)S(1)}, bf16[16,896]{1,0:T(8,128)(2,1)}, u32[]{:S(2)}) %copy-start.5) | copy-done | bytes 28696
  8.8 61.2 %shard_map.91 = bf16[1024,1024]{1,0:T(8,128)(2,1)S(1)} custom-call(bf16[1024,1024]{1,0:T(8,128)(2,1)S(1)} %copy-done, bf16[16,896]{1,0:T(8,128)(2,1)S(1)} %copy-done.5, s32[16,2]{1,0:T(8,128)S(1)} %copy.10.shard_ref, s32[16,2]{1,0:T(8,128)S(1)} %copy.11.row_ref, bf16[8,16,896]{2,1,0:T(8,128)(2,1)S(1)} %copy-done.4, bf16[1,896]{1,0:T(2,128)(2,1)S(1)} %reshape.3.gain_ref, ...), custom_call_target="tpu_custom_call" | custom-call | tf_op jit(solution)/shard_map/pallas_call | solution.py:425
  70.0 1.3 %copy.13 = bf16[1024,1024]{1,0:T(8,128)(2,1)} copy(bf16[1024,1024]{1,0:T(8,128)(2,1)S(1)} %shard_map.91) | data formatting | bytes 4194304
Async XLA Ops:
  2.2 1.6 %copy-start = (bf16[1024,1024]{1,0:T(8,128)(2,1)S(1)}, bf16[1024,1024]{1,0:T(8,128)(2,1)}, u32[]{:S(2)}) copy-start(bf16[1024,1024]{1,0:T(8,128)(2,1)} %queries_hbm.1) | copy-start | bytes 6291460
  3.8 1.1 %copy-start.1 = (bf16[448,896]{1,0:T(8,128)(2,1)S(1)}, bf16[448,896]{1,0:T(8,128)(2,1)}, u32[]{:S(2)}) copy-start(bf16[448,896]{1,0:T(8,128)(2,1)} %w_in_hbm.1) | copy-start | bytes 2408452
  4.9 1.1 %copy-start.2 = (bf16[448,896]{1,0:T(8,128)(2,1)S(1)}, bf16[448,896]{1,0:T(8,128)(2,1)}, u32[]{:S(2)}) copy-start(bf16[448,896]{1,0:T(8,128)(2,1)} %w_out_hbm.1) | copy-start | bytes 2408452
  6.1 1.0 %copy-start.3 = (bf16[2,112,1024]{2,1,0:T(8,128)(2,1)S(1)}, bf16[2,112,1024]{2,1,0:T(8,128)(2,1)}, u32[]{:S(2)}) copy-start(bf16[2,112,1024]{2,1,0:T(8,128)(2,1)} %w_kv_ref.1) | copy-start | bytes 1376260
  7.1 0.9 %copy-start.4 = (bf16[8,16,896]{2,1,0:T(8,128)(2,1)S(1)}, bf16[8,16,896]{2,1,0:T(8,128)(2,1)}, u32[]{:S(2)}) copy-start(bf16[8,16,896]{2,1,0:T(8,128)(2,1)} %db_ref.1) | copy-start | bytes 688132
  8.0 0.7 %copy-start.5 = (bf16[16,896]{1,0:T(8,128)(2,1)S(1)}, bf16[16,896]{1,0:T(8,128)(2,1)}, u32[]{:S(2)}) copy-start(bf16[16,896]{1,0:T(8,128)(2,1)} %cond_ref.1) | copy-start | bytes 86020

commit v2 on v1

--- a/solution.py
+++ b/solution.py
@@ -79,9 +79,9 @@
 
 
 def fused_kernel(
-    queries_hbm, cond_ref, shard_ref, row_ref, db_ref, gain_ref, w_in_hbm, w_out_hbm, w_kv_ref,
+    queries_hbm, cond_hbm, shard_ref, row_ref, db_ref, gain_hbm, w_in_hbm, w_out_hbm, w_kv_ref,
     out_ref,
-    wbuf, dbp, condf, xs, xv, nv, enc, part_send, part_recv, own_sum, y_send, y_recv,
+    wbuf, dbp, cond_ref, gain_ref, condf, xs, xv, keys, values, enc, part_send, part_recv, own_sum, y_send, y_recv,
     q_ref, w_in_ref, w_out_ref,
     local_sem, db_send, db_recv, w_send, w_recv, xs_send, xs_recv, sum_send, sum_recv,
 ):
@@ -95,7 +95,6 @@
     stored = db_ref.shape[0]
     depth = w_kv_ref.shape[1]
     rows = enc.shape[0]
-    half = rows // 2
     e = enc.shape[1]
     off = pl.multiple_of(jnp.minimum(t * WIDE, e - WIDE), 128)
 
@@ -108,6 +107,11 @@
         pltpu.make_async_copy(w_in_hbm, w_in_ref, local_sem.at[0]),
         pltpu.make_async_copy(w_out_hbm, w_out_ref, local_sem.at[1]),
         pltpu.make_async_copy(queries_hbm, q_ref, local_sem.at[2]),
+        pltpu.make_async_copy(gain_hbm, gain_ref, local_sem.at[3]),
+        pltpu.make_async_copy(cond_hbm.at[:, pl.ds(off, WIDE)], cond_ref, local_sem.at[4]),
+        pltpu.make_async_copy(
+            db_ref.at[:, :, pl.ds(off, WIDE)], dbp.at[pl.ds(s * stored, stored)], local_sem.at[5]
+        ),
     ]
     for load in loads:
         load.start()
@@ -194,133 +198,128 @@
 
         lax.fori_loop(first, last, one, 0)
 
-    condf[...] = cond_ref[:, pl.ds(off, WIDE)].astype(jnp.float32)
-    dbp[pl.ds(s * stored, stored)] = db_ref[:, :, pl.ds(off, WIDE)]
+    for load in loads[3:]:
+        load.wait()
+    condf[...] = cond_ref[...].astype(jnp.float32)
     for i in range(1, 8):
         db_arrival(i).wait()
 
+    blocks = rows // 128
+
+    def at_row(i):
+        return pl.ds(i * 128, 128)
+
+    def xs_copy(quarter, r, target, number):
+        return pltpu.make_async_remote_copy(
+            src_ref=xs.at[quarter, at_row(r)],
+            dst_ref=xs.at[quarter, at_row(r)],
+            send_sem=xs_send.at[number, r],
+            recv_sem=xs_recv.at[quarter, r],
+            device_id=(s, target),
+            device_id_type=MESH,
+        )
+
+    def xs_arrival(quarter, r):
+        here = xs.at[quarter, at_row(r)]
+        return pltpu.make_async_copy(here, here, xs_recv.at[quarter, r])
+
     def pick(g, carry):
         for k in range(K):
-            at = shard_ref[g, k] * stored + row_ref[g, k]
+            at = shard_ref[k, g] * stored + row_ref[k, g]
             picked = dbp[at].astype(jnp.float32) + condf[pl.ds(g, 1), :]
             xs[t, pl.ds(pl.multiple_of((g * K + k) * NL, NL), NL), :] = picked.astype(jnp.bfloat16)
         return carry
 
-    lax.fori_loop(0, rows // (K * NL), pick, 0)
-
-    def xs_copy(quarter, target, number):
+    per_block = 128 // (K * NL)
+    for r in range(blocks):
+        lax.fori_loop(r * per_block, (r + 1) * per_block, pick, 0)
+        xs_copy(t, r, ypeer, 0).start()
+        xs_copy(t, r, sib, 1).start()
+
+    gain = gain_ref[...].astype(jnp.float32).reshape(1, e)
+    theirs = (1 - core) * 64
+    mine = core * 64
+
+    def rows_of(r, inner):
+        return pl.ds(pl.multiple_of(r * 128 + inner, 64), 64)
+
+    def sum_copy(src, dst, target, number, r):
         return pltpu.make_async_remote_copy(
-            src_ref=xs.at[quarter],
-            dst_ref=xs.at[quarter],
-            send_sem=xs_send.at[number],
-            recv_sem=xs_recv.at[quarter],
+            src_ref=src,
+            dst_ref=dst,
+            send_sem=sum_send.at[number, r],
+            recv_sem=sum_recv.at[number, r],
             device_id=(s, target),
             device_id_type=MESH,
         )
 
-    def xs_arrival(quarter):
-        return pltpu.make_async_copy(xs.at[quarter], xs.at[quarter], xs_recv.at[quarter])
-
-    xs_copy(t, ypeer, 0).start()
-    xs_copy(t, sib, 1).start()
-    pass_on(1, 0, PIECES // 2)
-    xs_arrival(ypeer).wait()
-    xs_copy(ypeer, sib, 2).start()
-    pass_on(1, PIECES // 2, PIECES)
-    xs_arrival(sib).wait()
-    xs_arrival((sib + 2) % 4).wait()
-
-    gain = gain_ref[...].astype(jnp.float32)
-
-    def norm(i, carry):
-        at = pl.ds(pl.multiple_of(i * 64, 64), 64)
+    def to_sib(r):
+        return sum_copy(part_send.at[r], part_recv.at[r], sib, 0, r)
+
+    def to_y(r):
+        return sum_copy(y_send.at[r], y_recv.at[r], ypeer, 1, r)
+
+    def to_share(r):
+        return sum_copy(enc.at[rows_of(r, mine)], enc.at[rows_of(r, mine)], sib, 2, r)
+
+    def share_arrival(r):
+        here = enc.at[rows_of(r, theirs)]
+        return pltpu.make_async_copy(here, here, sum_recv.at[2, r])
+
+    def relay(r):
+        xs_arrival(ypeer, r).wait()
+        xs_copy(ypeer, r, sib, 2).start()
+
+    def feed_forward(r):
+        xs_arrival(sib, r).wait()
+        xs_arrival((sib + 2) % 4, r).wait()
+        at = at_row(r)
         whole = jnp.concatenate(
             [xs[0, at, :], xs[1, at, :], xs[2, at, :], xs[3, at, pl.ds(4 * WIDE - e, e - 3 * WIDE)]], axis=1
         )
         xv[at, :] = whole
         wide = whole.astype(jnp.float32)
         mean_square = jnp.mean(wide * wide, axis=1, keepdims=True)
-        nv[at, :] = (wide * lax.rsqrt(mean_square + 1e-06) * gain).astype(jnp.bfloat16)
-        return carry
-
-    lax.fori_loop(0, rows // 64, norm, 0)
+        normed = (wide * lax.rsqrt(mean_square + 1e-06) * gain).astype(jnp.bfloat16)
+        pre_act = lax.dot_general(
+            normed, w_in_ref[...], (((1,), (1,)), ((), ())), preferred_element_type=jnp.float32
+        )
+        hidden = jax.nn.gelu(pre_act).astype(jnp.bfloat16)
+        own_sum[at, :] = jnp.dot(hidden, w_out_ref[...], preferred_element_type=jnp.float32)
+        part_send[r] = own_sum[rows_of(r, theirs), :].astype(jnp.bfloat16)
+        to_sib(r).start()
+
+    def add_sib(r):
+        to_sib(r).wait_recv()
+        own = own_sum[rows_of(r, mine), :] + part_recv[r].astype(jnp.float32)
+        own_sum[rows_of(r, mine), :] = own
+        y_send[r] = own.astype(jnp.bfloat16)
+        to_y(r).start()
+
+    def share(r):
+        to_y(r).wait_recv()
+        where = rows_of(r, mine)
+        total = own_sum[where, :] + y_recv[r].astype(jnp.float32)
+        enc[where, :] = (xv[where, :].astype(jnp.float32) + total).astype(jnp.bfloat16)
+        to_share(r).start()
+
     loads[0].wait()
     loads[1].wait()
-
-    def ffn(first):
-        block = nv[pl.ds(pl.multiple_of(first, 128), 128), :]
-        pre_act = lax.dot_general(
-            block, w_in_ref[...], (((1,), (1,)), ((), ())), preferred_element_type=jnp.float32
-        )
-        hidden = jax.nn.gelu(pre_act).astype(jnp.bfloat16)
-        return jnp.dot(hidden, w_out_ref[...], preferred_element_type=jnp.float32)
-
-    def sum_copy(src, dst, target, number):
-        return pltpu.make_async_remote_copy(
-            src_ref=src,
-            dst_ref=dst,
-            send_sem=sum_send.at[number],
-            recv_sem=sum_recv.at[number],
-            device_id=(s, target),
-            device_id_type=MESH,
-        )
-
-    theirs = (1 - core) * half
-    mine = core * half
-    steps = half // 128
-
-    def at_row(i):
-        return pl.ds(pl.multiple_of(i * 128, 128), 128)
-
-    def to_sib(i):
-        return sum_copy(part_send.at[at_row(i)], part_recv.at[at_row(i)], sib, i)
-
-    def to_y(i):
-        return sum_copy(y_send.at[at_row(i)], y_recv.at[at_row(i)], ypeer, steps + i)
-
-    def to_share(i):
-        where = pl.ds(pl.multiple_of(mine + i * 128, 128), 128)
-        return sum_copy(enc.at[where], enc.at[where], sib, 2 * steps + i)
-
-    def share_arrival(i):
-        where = pl.ds(pl.multiple_of(theirs + i * 128, 128), 128)
-        return pltpu.make_async_copy(enc.at[where], enc.at[where], sum_recv.at[2 * steps + i])
-
-    def send_theirs(i, carry):
-        part_send[at_row(i), :] = ffn(theirs + i * 128).astype(jnp.bfloat16)
-        to_sib(i).start()
-        return carry
-
-    lax.fori_loop(0, steps, send_theirs, 0)
-
-    def send_mine(i, carry):
-        own = ffn(mine + i * 128)
-        to_sib(i).wait_recv()
-        own = own + part_recv[at_row(i), :].astype(jnp.float32)
-        own_sum[at_row(i), :] = own
-        y_send[at_row(i), :] = own.astype(jnp.bfloat16)
-        to_y(i).start()
-        return carry
-
-    lax.fori_loop(0, steps, send_mine, 0)
-    pass_on(2, 0, PIECES)
-
-    def share_mine(i, carry):
-        where = pl.ds(pl.multiple_of(mine + i * 128, 128), 128)
-        to_y(i).wait_recv()
-        total = own_sum[at_row(i), :] + y_recv[at_row(i), :].astype(jnp.float32)
-        enc[where, :] = (xv[where, :].astype(jnp.float32) + total).astype(jnp.bfloat16)
-        to_share(i).start()
-        return carry
-
-    lax.fori_loop(0, steps, share_mine, 0)
-    pass_on(3, 0, PIECES)
-
-    def await_share(i, carry):
-        share_arrival(i).wait()
-        return carry
-
-    lax.fori_loop(0, steps, await_share, 0)
+    relay(0)
+    for r in range(blocks):
+        if r + 1 < blocks:
+            relay(r + 1)
+        feed_forward(r)
+        if r:
+            add_sib(r - 1)
+        pass_on(1, 2 * r, 2 * r + 2)
+    add_sib(blocks - 1)
+    for r in range(blocks):
+        pass_on(2, 2 * r, 2 * r + 2)
+        share(r)
+    pass_on(3, 0, 4)
+    for r in range(blocks):
+        share_arrival(r).wait()
     loads[2].wait()
 
     span = 4 * K * NL
@@ -328,55 +327,50 @@
     tall = lax.broadcasted_iota(jnp.int32, (qspan, span), 0) // GROUP
     flat = lax.broadcasted_iota(jnp.int32, (qspan, span), 1) // (K * NL)
     inside = tall == flat
-    scale = HEAD ** -0.5
+    scale = HEAD ** -0.5 * 1.4426950408889634
     ones = jnp.ones((span, HEAD), jnp.bfloat16)
 
     def chunk(c, carry):
         for j in range(2):
             p = 2 * c + j
             pltpu.make_async_copy(own_piece(p), slot(p, s), w_recv.at[p, s]).wait()
+
             for i in range(ACROSS):
                 w_arrival(p, 2 * i + 1 - x).wait()
 
-        def quad(i, inner):
-            krows = pl.ds(pl.multiple_of(i * span, span), span)
-            qrows = pl.ds(pl.multiple_of(i * qspan, qspan), qspan)
-            block = enc[krows, :]
-            keys = jnp.dot(block, wbuf[2 * c], preferred_element_type=jnp.float32).astype(jnp.bfloat16)
-            values = jnp.dot(block, wbuf[2 * c + 1], preferred_element_type=jnp.float32).astype(jnp.bfloat16)
-            for h in range(WIDE // HEAD):
-                cols = pl.ds(pl.multiple_of(c * WIDE + h * HEAD, HEAD), HEAD)
-                query = q_ref[qrows, cols]
+        pass_on(3, jnp.minimum(2 * c + 4, PIECES), jnp.minimum(2 * c + 6, PIECES))
+        block = enc[...]
+        keys[...] = jnp.dot(block, wbuf[2 * c], preferred_element_type=jnp.float32).astype(jnp.bfloat16)
+        values[...] = jnp.dot(block, wbuf[2 * c + 1], preferred_element_type=jnp.float32).astype(jnp.bfloat16)
+        for h in range(WIDE // HEAD):
+            cols = pl.ds(pl.multiple_of(c * WIDE + h * HEAD, HEAD), HEAD)
+            part = slice(h * HEAD, (h + 1) * HEAD)
+            for i in range(rows // span):
+                krows = slice(i * span, (i + 1) * span)
+                qrows = slice(i * qspan, (i + 1) * qspan)
                 scores = lax.dot_general(
-                    query, keys[:, h * HEAD : (h + 1) * HEAD], (((1,), (1,)), ((), ())),
+                    q_ref[qrows, cols], keys[krows, part], (((1,), (1,)), ((), ())),
                     preferred_element_type=jnp.float32,
                 )
                 scores = jnp.where(inside, scores * scale, -jnp.inf)
                 top = jnp.max(scores, axis=1, keepdims=True)
-                grown = jnp.exp(scores - top).astype(jnp.bfloat16)
-                both = jnp.concatenate([values[:, h * HEAD : (h + 1) * HEAD], ones], axis=1)
+                grown = jnp.exp2(scores - top).astype(jnp.bfloat16)
+                both = jnp.concatenate([values[krows, part], ones], axis=1)
                 mixed = jnp.dot(grown, both, preferred_element_type=jnp.float32)
                 out_ref[qrows, cols] = (mixed[:, :HEAD] / mixed[:, HEAD:]).astype(jnp.bfloat16)
-            return inner
-
-        lax.fori_loop(0, rows // span, quad, 0)
         return carry
 
     lax.fori_loop(0, PIECES // 2, chunk, 0)
 
     for i in range(1, 8):
         db_copy(i).wait_send()
-    xs_copy(t, ypeer, 0).wait_send()
-    xs_copy(t, sib, 1).wait_send()
-    xs_copy(ypeer, sib, 2).wait_send()
-
-    def sums_done(i, carry):
-        to_sib(i).wait_send()
-        to_y(i).wait_send()
-        to_share(i).wait_send()
-        return carry
-
-    lax.fori_loop(0, steps, sums_done, 0)
+    for r in range(blocks):
+        xs_copy(t, r, ypeer, 0).wait_send()
+        xs_copy(t, r, sib, 1).wait_send()
+        xs_copy(ypeer, r, sib, 2).wait_send()
+        to_sib(r).wait_send()
+        to_y(r).wait_send()
+        to_share(r).wait_send()
 
     def sends_done(p, carry):
         w_copy(own_piece(p), p, s, 0).wait_send()
@@ -389,24 +383,26 @@
         def _():
             w_copy(own_piece(p), p, s, 2).wait_send()
 
-        for hop in range(1, ACROSS):
-            @pl.when(z >= hop)
-            def _():
-                b = s - 2 * hop
-                w_copy(slot(p, b), p, b, 0).wait_send()
-
-                @pl.when(z < ACROSS - 1)
+        @pl.when(p >= 0)
+        def _():
+            for hop in range(1, ACROSS):
+                @pl.when(z >= hop)
                 def _():
-                    w_copy(slot(p, b), p, b, 1).wait_send()
-
-            @pl.when(z + hop < ACROSS)
-            def _():
-                b = s + 2 * hop
-                w_copy(slot(p, b), p, b, 0).wait_send()
-
-                @pl.when(z > 0)
+                    b = s - 2 * hop
+                    w_copy(slot(p, b), p, b, 0).wait_send()
+
+                    @pl.when(z < ACROSS - 1)
+                    def _():
+                        w_copy(slot(p, b), p, b, 1).wait_send()
+
+                @pl.when(z + hop < ACROSS)
                 def _():
-                    w_copy(slot(p, b), p, b, 2).wait_send()
+                    b = s + 2 * hop
+                    w_copy(slot(p, b), p, b, 0).wait_send()
+
+                    @pl.when(z > 0)
+                    def _():
+                        w_copy(slot(p, b), p, b, 2).wait_send()
 
         return carry
 
@@ -416,47 +412,49 @@
 def fused_body(queries, group_cond, nbr_shard, nbr_row, database, enc_gain, w_in, w_out, w_kv):
     bf16, f32 = jnp.bfloat16, jnp.float32
     rows = nbr_shard.shape[0] * K * NL
-    half = rows // 2
-    steps = half // 128
+    blocks = rows // 128
     vmem = pl.BlockSpec(memory_space=pltpu.VMEM)
     smem = pl.BlockSpec(memory_space=pltpu.SMEM)
-    anywhere = pl.BlockSpec(memory_space=pl.ANY)
+    hbm = pl.BlockSpec(memory_space=pltpu.HBM)
     dma = pltpu.SemaphoreType.DMA
     return pl.pallas_call(
         fused_kernel,
         out_shape=jax.ShapeDtypeStruct(queries.shape, bf16),
-        in_specs=[anywhere, vmem, smem, smem, vmem, vmem, anywhere, anywhere, vmem],
+        in_specs=[hbm, hbm, smem, smem, hbm, hbm, hbm, hbm, hbm],
         out_specs=vmem,
         scratch_shapes=[
             pltpu.VMEM((PIECES, E, WIDE), bf16),
             pltpu.VMEM((8 * database.shape[0], NL, WIDE), bf16),
+            pltpu.VMEM((group_cond.shape[0], WIDE), bf16),
+            pltpu.VMEM(enc_gain.shape, bf16),
             pltpu.VMEM((group_cond.shape[0], WIDE), f32),
             pltpu.VMEM((4, rows, WIDE), bf16),
             pltpu.VMEM((rows, E), bf16),
+            pltpu.VMEM((rows, WIDE), bf16),
+            pltpu.VMEM((rows, WIDE), bf16),
             pltpu.VMEM((rows, E), bf16),
-            pltpu.VMEM((rows, E), bf16),
-            pltpu.VMEM((half, E), bf16),
-            pltpu.VMEM((half, E), bf16),
-            pltpu.VMEM((half, E), f32),
-            pltpu.VMEM((half, E), bf16),
-            pltpu.VMEM((half, E), bf16),
+            pltpu.VMEM((blocks, 64, E), bf16),
+            pltpu.VMEM((blocks, 64, E), bf16),
+            pltpu.VMEM((rows, E), f32),
+            pltpu.VMEM((blocks, 64, E), bf16),
+            pltpu.VMEM((blocks, 64, E), bf16),
             pltpu.VMEM(queries.shape, bf16),
             pltpu.VMEM(w_in.shape, bf16),
             pltpu.VMEM(w_out.shape, bf16),
-            dma((3,)),
+            dma((6,)),
             dma((8,)),
             dma((8,)),
             dma((3, PIECES, 8)),
             dma((PIECES, 8)),
-            dma((3,)),
-            dma((4,)),
-            dma((3 * steps,)),
-            dma((3 * steps,)),
+            dma((3, blocks)),
+            dma((4, blocks)),
+            dma((3, blocks)),
+            dma((3, blocks)),
         ],
         compiler_params=pltpu.CompilerParams(
-            collective_id=0, has_side_effects=True, vmem_limit_bytes=40 * 1024 * 1024
+            collective_id=0, has_side_effects=True, vmem_limit_bytes=62 * 1024 * 1024
         ),
-    )(queries, group_cond, nbr_shard, nbr_row, database, enc_gain.reshape(1, E), w_in, w_out, w_kv)
+    )(queries, group_cond, nbr_shard.T, nbr_row.T, database, enc_gain, w_in, w_out, w_kv)
 
 
 def solution(mesh):

time: 71.7 us -> 65.6 us (0.915)
  local copies, waits for them, and re-layouts: 10.1 us -> 3.08 us
  Pallas kernels: 61.2 us -> 62 us
    unnamed x15 -> x1, local copies, waits for them, and re-layouts: 9.4 us -> 3.08 us
    pallas_call x1, Pallas kernels: 61.2 us -> 62 us  [fused_body(): pl.pallas_call(fused_kernel, out_shape=jax.ShapeDtypeStruct(queries.shape...]
where the time goes in v2:
time: 65.6 us; the launch traced here: 65.1 us
  Pallas kernels  62 us (95%)
  local copies, waits for them, and re-layouts  3.08 us (5%)
    pallas_call x1, Pallas kernels, fused_body(): pl.pallas_call(fused_kernel, out_shape=jax.ShapeDtypeStruct(queries.shape...  62 us
    unnamed x1, local copies, waits for them, and re-layouts  3.08 us

profile of v2, /device:TPU:0, one launch (start us, length us, event | category | flops | bytes accessed | tf_op | source)
XLA Modules:
  0.0 65.1 jit_solution(7010828263499843910)
XLA Ops:
  0.0 62.0 %shard_map.91 = bf16[1024,1024]{1,0:T(8,128)(2,1)} custom-call(bf16[1024,1024]{1,0:T(8,128)(2,1)} %queries_hbm.1, bf16[16,896]{1,0:T(8,128)(2,1)} %cond_hbm.1, s32[2,16]{1,0:T(2,128)} %bitcast.2, s32[2,16]{1,0:T(2,128)} %bitcast.3, bf16[8,16,896]{2,1,0:T(8,128)(2,1)} %db_ref.1, bf16[896]{0:T(1024)(128)(2,1)} %gain_hbm.1, bf16[448,896]{1,0:T(8,128)(2,1)} %w_in_hbm.1, ...), custom_call_target="tpu_custom_call" | custom-call | tf_op jit(solution)/shard_map/pallas_call | solution.py:420
  62.0 3.1 %copy.11 = bf16[1024,1024]{1,0:T(8,128)(2,1)} copy(bf16[1024,1024]{1,0:T(8,128)(2,1)} %shard_map.91) | data formatting | bytes 4194304

commit v3 on v2

--- a/solution.py
+++ b/solution.py
@@ -117,24 +117,67 @@
         load.start()
     pl.semaphore_wait(barrier, 9)
 
-    def db_copy(i):
+    def db_slot(b):
+        return dbp.at[pl.ds(b * stored, stored)]
+
+    def db_copy(src, b, way):
+        target = (flip, s + 2, s - 2)[way]
         return pltpu.make_async_remote_copy(
-            src_ref=db_ref.at[:, :, pl.ds(off, WIDE)],
-            dst_ref=dbp.at[pl.ds(s * stored, stored)],
-            send_sem=db_send.at[i],
-            recv_sem=db_recv.at[i],
-            device_id=((s + i) % 8, t),
+            src_ref=src,
+            dst_ref=db_slot(b),
+            send_sem=db_send.at[way, b],
+            recv_sem=db_recv.at[b],
+            device_id=(target, t),
             device_id_type=MESH,
         )
 
-    def db_arrival(i):
-        source = (s + 8 - i) % 8
-        return pltpu.make_async_copy(
-            dbp.at[pl.ds(source * stored, stored)], dbp.at[pl.ds(source * stored, stored)], db_recv.at[i]
-        )
-
-    for i in range(1, 8):
-        db_copy(i).start()
+    def db_arrival(b):
+        return pltpu.make_async_copy(db_slot(b), db_slot(b), db_recv.at[b])
+
+    def db_own(finish):
+        own = db_ref.at[:, :, pl.ds(off, WIDE)]
+
+        def do(copy):
+            if finish:
+                copy.wait_send()
+            else:
+                copy.start()
+
+        @pl.when(z < ACROSS - 1)
+        def _():
+            do(db_copy(own, s, 1))
+
+        @pl.when(z > 0)
+        def _():
+            do(db_copy(own, s, 2))
+
+        do(db_copy(own, s, 0))
+
+    def db_pass(hop, finish):
+        for reached, b, further, way in (
+            (z >= hop, s - 2 * hop, z < ACROSS - 1, 1),
+            (z + hop < ACROSS, s + 2 * hop, z > 0, 2),
+        ):
+            @pl.when(reached)
+            def _():
+                if not finish:
+                    db_arrival(b).wait()
+
+                @pl.when(further)
+                def _():
+                    copy = db_copy(db_slot(b), b, way)
+                    if finish:
+                        copy.wait_send()
+                    else:
+                        copy.start()
+
+                copy = db_copy(db_slot(b), b, 0)
+                if finish:
+                    copy.wait_send()
+                else:
+                    copy.start()
+
+    db_own(False)
 
     def slot(p, b):
         return wbuf.at[p, pl.ds(pl.multiple_of(b * depth, 16), depth), :]
@@ -170,7 +213,25 @@
         pltpu.make_async_copy(own_piece(p), slot(p, s), w_recv.at[p, s]).start()
         return carry
 
-    lax.fori_loop(0, PIECES, own_start, 0)
+    lax.fori_loop(0, 1, own_start, 0)
+
+    def x_first(hop, finish):
+        moves = [(z >= hop, -2 * hop, (1,)), (z + hop < ACROSS, 2 * hop, (2,))] if hop else [(z >= 0, 0, (1, 2))]
+        for reached, shift, ways in moves:
+            @pl.when(reached)
+            def _():
+                for base in (s, flip) if hop else (flip,):
+                    b = base + shift
+                    if not finish:
+                        w_arrival(0, b).wait()
+                    for way in ways:
+                        @pl.when(z < ACROSS - 1 if way == 1 else z > 0)
+                        def _():
+                            copy = w_copy(slot(0, b), 0, b, way)
+                            if finish:
+                                copy.wait_send()
+                            else:
+                                copy.start()
 
     def pass_on(hop, first, last):
         def one(p, carry):
@@ -201,8 +262,11 @@
     for load in loads[3:]:
         load.wait()
     condf[...] = cond_ref[...].astype(jnp.float32)
-    for i in range(1, 8):
-        db_arrival(i).wait()
+    for hop in range(1, ACROSS):
+        db_pass(hop, False)
+    lax.fori_loop(1, PIECES, own_start, 0)
+    for i in range(ACROSS):
+        db_arrival(2 * i + 1 - x).wait()
 
     blocks = rows // 128
 
@@ -235,6 +299,7 @@
         lax.fori_loop(r * per_block, (r + 1) * per_block, pick, 0)
         xs_copy(t, r, ypeer, 0).start()
         xs_copy(t, r, sib, 1).start()
+    x_first(0, False)
 
     gain = gain_ref[...].astype(jnp.float32).reshape(1, e)
     theirs = (1 - core) * 64
@@ -306,18 +371,21 @@
     loads[0].wait()
     loads[1].wait()
     relay(0)
+    x_first(1, False)
     for r in range(blocks):
         if r + 1 < blocks:
             relay(r + 1)
         feed_forward(r)
         if r:
             add_sib(r - 1)
-        pass_on(1, 2 * r, 2 * r + 2)
+        pass_on(1, 1 + 2 * r, min(3 + 2 * r, PIECES))
     add_sib(blocks - 1)
+    x_first(2, False)
     for r in range(blocks):
-        pass_on(2, 2 * r, 2 * r + 2)
+        pass_on(2, 1 + 2 * r, min(3 + 2 * r, PIECES))
         share(r)
-    pass_on(3, 0, 4)
+    x_first(3, False)
+    pass_on(3, 1, 4)
     for r in range(blocks):
         share_arrival(r).wait()
     loads[2].wait()
@@ -335,8 +403,10 @@
             p = 2 * c + j
             pltpu.make_async_copy(own_piece(p), slot(p, s), w_recv.at[p, s]).wait()
 
-            for i in range(ACROSS):
-                w_arrival(p, 2 * i + 1 - x).wait()
+            @pl.when(p > 0)
+            def _():
+                for i in range(ACROSS):
+                    w_arrival(p, 2 * i + 1 - x).wait()
 
         pass_on(3, jnp.minimum(2 * c + 4, PIECES), jnp.minimum(2 * c + 6, PIECES))
         block = enc[...]
@@ -362,8 +432,9 @@
 
     lax.fori_loop(0, PIECES // 2, chunk, 0)
 
-    for i in range(1, 8):
-        db_copy(i).wait_send()
+    db_own(True)
+    for hop in range(1, ACROSS):
+        db_pass(hop, True)
     for r in range(blocks):
         xs_copy(t, r, ypeer, 0).wait_send()
         xs_copy(t, r, sib, 1).wait_send()
@@ -372,6 +443,9 @@
         to_y(r).wait_send()
         to_share(r).wait_send()
 
+    for hop in range(ACROSS):
+        x_first(hop, True)
+
     def sends_done(p, carry):
         w_copy(own_piece(p), p, s, 0).wait_send()
 
@@ -383,7 +457,7 @@
         def _():
             w_copy(own_piece(p), p, s, 2).wait_send()
 
-        @pl.when(p >= 0)
+        @pl.when(p > 0)
         def _():
             for hop in range(1, ACROSS):
                 @pl.when(z >= hop)
@@ -442,7 +516,7 @@
             pltpu.VMEM(w_in.shape, bf16),
             pltpu.VMEM(w_out.shape, bf16),
             dma((6,)),
-            dma((8,)),
+            dma((3, 8)),
             dma((8,)),
             dma((3, PIECES, 8)),
             dma((PIECES, 8)),

time: 65.6 us -> 64.9 us (0.989)
  no operation moved by 1% of the time
where the time goes in v3:
time: 64.9 us; the launch traced here: 64.7 us
  Pallas kernels  61.6 us (95%)
  local copies, waits for them, and re-layouts  3.08 us (5%)
    pallas_call x1, Pallas kernels, fused_body(): pl.pallas_call(fused_kernel, out_shape=jax.ShapeDtypeStruct(queries.shape...  61.6 us
    unnamed x1, local copies, waits for them, and re-layouts  3.08 us

profile of v3, /device:TPU:0, one launch (start us, length us, event | category | flops | bytes accessed | tf_op | source)
XLA Modules:
  0.0 64.7 jit_solution(8105587436789991813)
XLA Ops:
  0.0 61.6 %shard_map.91 = bf16[1024,1024]{1,0:T(8,128)(2,1)} custom-call(bf16[1024,1024]{1,0:T(8,128)(2,1)} %queries_hbm.1, bf16[16,896]{1,0:T(8,128)(2,1)} %cond_hbm.1, s32[2,16]{1,0:T(2,128)} %bitcast.2, s32[2,16]{1,0:T(2,128)} %bitcast.3, bf16[8,16,896]{2,1,0:T(8,128)(2,1)} %db_ref.1, bf16[896]{0:T(1024)(128)(2,1)} %gain_hbm.1, bf16[448,896]{1,0:T(8,128)(2,1)} %w_in_hbm.1, ...), custom_call_target="tpu_custom_call" | custom-call | tf_op jit(solution)/shard_map/pallas_call | solution.py:494
  61.7 3.1 %copy.11 = bf16[1024,1024]{1,0:T(8,128)(2,1)} copy(bf16[1024,1024]{1,0:T(8,128)(2,1)} %shard_map.91) | data formatting | bytes 4194304
